TPU v7x, 32 devices: a whole 2x2x4 slice. The times are simulated.
32 devices in a mesh: grp: 2 (over y), ori: 4 (over z), ty: 2 (over x), tx: 2 (over core).
Axes of the slice: x: 2, y: 2, z: 4, core: 2. Of those that a mesh axis runs over, the one named last changes fastest.
Arguments:
- volume: float32 [32, 32, 64], P(('grp', 'ty'), 'tx'), parts along dimension 0, may hold values from -1000 to 1000
- templates: bfloat16 [128, 1728], P(('grp', 'ori')), parts along dimension 0, may hold values from -1 to 1, as said below
- prior_table: int32 [64], P('ori'), may hold values from 0 to 7
- moment_table: float32 [4, 64], P(None, 'ori'), may hold values from -6 to 6
Outputs:
- log_total: float32 [32, 32, 64], P(('grp', 'ty'), ('tx', 'ori')), parts along dimension 0
- moments: float32 [4, 32, 32, 64], P(None, ('grp', 'ty'), ('tx', 'ori')), parts along dimension 1
There are 2 independent parts, one for each index of `grp`. A program takes and returns all parts, laid end to end along the dimension named above; an argument that names none is the same for every part. Nothing has to cross between parts.
Inputs may be any that keep to these rules, and one draw needn't show every extreme that they name: `templates`: each row has unit Euclidean norm up to rounding.
All inputs are finite; a program needn't handle non-finite values.
Results may differ from a plain program's by a relative error of at most 0.0073.
Values may be sent and summed in bfloat16 or wider, within the bound.
A program may use at most 64 MiB of HBM per device.

v0:
```python
import functools

import jax
import jax.numpy as jnp
from jax import lax
from jax.experimental import pallas as pl
from jax.experimental.pallas import tpu as pltpu
from jax.sharding import PartitionSpec as P

score_scale = 7.0
prior_step = 0.5
epsilon = 1e-05
MESH = pl.DeviceIdType.MESH
f32 = jnp.float32
bf16 = jnp.bfloat16
EDGE = 8
WIDE = 24


def iota(shape, dim):
    return lax.broadcasted_iota(jnp.int32, shape, dim)


def kernel(
    n_ori, n_ty, own,
    vol_ref, tmpl_ref, prior_ref, mom_ref, out_ref,
    ext, tall, aux, shifts, grid_ref, weights,
    vol_send, vol_recv, tmpl_send, tmpl_recv, aux_send, aux_recv,
):
    rows, cols, z_cells = vol_ref.shape
    orients = tmpl_ref.shape[0]
    all_orients = n_ori * orients
    ori = lax.axis_index("ori")
    ty = lax.axis_index("ty")
    tx = lax.axis_index("tx")
    has_prev = ty > 0
    has_next = ty < n_ty - 1
    other = 1 - tx
    pairs = (own + 1) // 2

    barrier = pltpu.get_barrier_semaphore()
    for k in range(1, n_ori):
        pl.semaphore_signal(
            barrier, inc=1, device_id={"ori": lax.rem(ori + k, n_ori)}, device_id_type=MESH
        )
    pl.semaphore_signal(barrier, inc=1, device_id={"tx": other}, device_id_type=MESH)

    @pl.when(has_prev)
    def _():
        pl.semaphore_signal(barrier, inc=1, device_id={"ty": ty - 1}, device_id_type=MESH)
        pl.semaphore_signal(
            barrier, inc=1, device_id={"ty": ty - 1, "tx": other}, device_id_type=MESH
        )

    @pl.when(has_next)
    def _():
        pl.semaphore_signal(barrier, inc=1, device_id={"ty": ty + 1}, device_id_type=MESH)
        pl.semaphore_signal(
            barrier, inc=1, device_id={"ty": ty + 1, "tx": other}, device_id_type=MESH
        )

    lanes = aux.shape[2]
    place = (iota((orients, lanes), 1) == iota((orients, lanes), 0) + ori * orients).astype(f32)
    small = jnp.concatenate(
        [mom_ref[...], prior_ref[...].astype(f32), jnp.zeros((3, orients), f32)], axis=0
    )
    aux[ori] = jnp.dot(small, place, precision=lax.Precision.HIGHEST, preferred_element_type=f32)
    own_cols = pl.ds(pl.multiple_of(EDGE + tx * cols, 8), cols)

    greeted = n_ori + jnp.where(has_prev, 2, 0) + jnp.where(has_next, 2, 0)
    pl.semaphore_wait(barrier, greeted)

    edge_src = pl.ds(pl.multiple_of((1 - tx) * (cols - 8), 8), 8)
    edge_dst = pl.ds(pl.multiple_of(EDGE + tx * cols + (1 - tx) * (cols - 8), 8), 8)

    def vol_copy(slot, whole, row, device):
        return pltpu.make_async_remote_copy(
            src_ref=vol_ref if whole else vol_ref.at[:, edge_src, :],
            dst_ref=ext.at[pl.ds(row, rows), own_cols if whole else edge_dst, :],
            send_sem=vol_send.at[slot],
            recv_sem=vol_recv.at[slot],
            device_id=device,
            device_id_type=MESH,
        )

    to_core = vol_copy(0, False, rows, {"tx": other})
    to_next = vol_copy(1, True, 0, {"ty": ty + 1})
    to_next_x = vol_copy(2, False, 0, {"ty": ty + 1, "tx": other})
    to_prev = vol_copy(3, True, 2 * rows, {"ty": ty - 1})
    to_prev_x = vol_copy(4, False, 2 * rows, {"ty": ty - 1, "tx": other})

    @pl.when(has_next)
    def _():
        to_next.start()
        to_next_x.start()

    @pl.when(has_prev)
    def _():
        to_prev.start()
        to_prev_x.start()

    to_core.start()
    gathers = []
    for k in sorted(range(1, n_ori), key=lambda k: -min(k, n_ori - k)):
        target = {"ori": lax.rem(ori + k, n_ori)}
        for src, dst, ssem, rsem in (
            (tmpl_ref, tall.at[ori], tmpl_send, tmpl_recv),
            (aux.at[ori], aux.at[ori], aux_send, aux_recv),
        ):
            copy = pltpu.make_async_remote_copy(
                src_ref=src, dst_ref=dst, send_sem=ssem.at[k - 1], recv_sem=rsem.at[k - 1],
                device_id=target, device_id_type=MESH,
            )
            copy.start()
            gathers.append(copy)

    tall[ori] = tmpl_ref[...]
    ext[pl.ds(rows, rows), own_cols, :] = vol_ref[...]
    edge = jnp.zeros((3 * rows, EDGE, z_cells), f32)
    ext[:, 0:EDGE, :] = edge
    ext[:, EDGE + 2 * cols : EDGE + 2 * cols + EDGE, :] = edge

    blank = jnp.zeros((rows, 2 * cols, z_cells), f32)

    @pl.when(jnp.logical_not(has_prev))
    def _():
        ext[0:rows, EDGE : EDGE + 2 * cols, :] = blank

    @pl.when(jnp.logical_not(has_next))
    def _():
        ext[2 * rows : 3 * rows, EDGE : EDGE + 2 * cols, :] = blank

    gap = iota((128, 128), 0) - iota((128, 128), 1)
    same = (iota((128, 128), 0) >= 64) == (iota((128, 128), 1) >= 64)
    for c in range(12):
        shifts[:, c * 128 : (c + 1) * 128] = ((gap == c - 5) & same).astype(f32).astype(bf16)
    row_id = iota((288, 384), 0)
    col_id = iota((288, 384), 1)
    half = jnp.where(col_id >= 192, 1, 0)
    within = col_id - 192 * half
    tap_b = within & 15
    perm = (
        (row_id == 144 * half + tap_b * 12 + (within >> 4)) & (tap_b < 12)
    ).astype(f32).astype(bf16)

    to_core.wait()

    @pl.when(has_next)
    def _():
        to_prev_in = vol_copy(3, True, 2 * rows, {"ty": ty + 1})
        to_prev_x_in = vol_copy(4, False, 2 * rows, {"ty": ty + 1, "tx": other})
        to_next.wait_send()
        to_next_x.wait_send()
        to_prev_in.wait_recv()
        to_prev_x_in.wait_recv()

    @pl.when(has_prev)
    def _():
        to_next_in = vol_copy(1, True, 0, {"ty": ty - 1})
        to_next_x_in = vol_copy(2, False, 0, {"ty": ty - 1, "tx": other})
        to_prev.wait_send()
        to_prev_x.wait_send()
        to_next_in.wait_recv()
        to_next_x_in.wait_recv()

    grid_rows = rows + 11
    x_first = tx * cols + ori * own
    raw = ext[1 : rows + 16, pl.ds(x_first + 1, WIDE), :]
    both = jnp.concatenate([raw, raw * raw], axis=-1)
    sums = both[0:grid_rows]
    for d in range(1, 5):
        sums = sums + both[d : d + grid_rows]
    flat = sums
    for d in range(1, 5):
        flat = flat + pltpu.roll(sums, WIDE - d, 1)
    lane = iota(flat.shape, 2) & 63
    total = flat
    for d in (1, 2):
        total = total + jnp.where(lane >= d, pltpu.roll(flat, d, 2), 0.0)
        total = total + jnp.where(lane < z_cells - d, pltpu.roll(flat, 128 - d, 2), 0.0)
    mean = total * (1.0 / 125.0)
    second = pltpu.roll(mean, 64, 2)
    centre = pltpu.roll(both[2 : 2 + grid_rows], WIDE - 2, 1)
    normed = (centre - mean) * lax.rsqrt(second - mean * mean + epsilon)
    y_at = iota(flat.shape, 0) + (ty * rows - 5)
    x_at = iota(flat.shape, 1)
    x_glob = x_at + (x_first - 5)
    inside = (y_at >= 0) & (y_at < n_ty * rows) & (x_glob >= 0) & (x_glob < 2 * cols)
    inside = inside & (x_at < own + 11) & (iota(flat.shape, 2) < z_cells)
    normed = jnp.where(inside, normed, 0.0).astype(bf16).astype(f32)
    blocks = []
    for p in range(pairs):
        block = normed[:, 2 * p : 2 * p + 16, :]
        if 2 * p + 1 < own:
            block = block + pltpu.roll(normed[:, 2 * p + 1 : 2 * p + 17, :], 64, 2)
        blocks.append(block.astype(bf16).reshape(grid_rows * 16, 128))
    stacked = jnp.concatenate(blocks, axis=0)
    for c in range(0, 12, 2):
        moved = jnp.dot(
            stacked, shifts[:, c * 128 : (c + 2) * 128], preferred_element_type=f32
        ).astype(bf16)
        for p in range(pairs):
            part = moved[p * grid_rows * 16 : (p + 1) * grid_rows * 16]
            for e in range(2):
                grid_ref[:, c + e, :, p * 128 : (p + 1) * 128] = part[
                    :, e * 128 : (e + 1) * 128
                ].reshape(grid_rows, 16, 128)

    for copy in gathers:
        copy.wait()
    cubes = tall[...].reshape(all_orients, 1728)
    for a in range(6):
        weights[:, a * 384 : (a + 1) * 384] = jnp.dot(
            cubes[:, a * 288 : (a + 1) * 288], perm, preferred_element_type=f32
        ).astype(bf16)
    table = jnp.sum(aux[...], axis=0)[:, 0:all_orients]
    eye = iota((all_orients, all_orients), 0) == iota((all_orients, all_orients), 1)
    prior = jnp.sum(jnp.where(eye, table[4:5], 0.0), axis=1, keepdims=True) * prior_step
    high = table[0:4].astype(bf16)
    low = (table[0:4] - high.astype(f32)).astype(bf16)
    factors = jnp.concatenate(
        [high.astype(f32), low.astype(f32), jnp.ones((8, all_orients), f32)], axis=0
    ).astype(bf16)
    for y in range(rows):
        window = grid_ref[y : y + 12].reshape(2304, pairs * 128)
        corr = jnp.dot(weights[...], window, preferred_element_type=f32)
        scores = score_scale * corr - prior
        peak = jnp.max(scores, axis=0, keepdims=True)
        terms = jnp.exp(scores - peak)
        log_total = peak + jnp.log(jnp.sum(terms, axis=0, keepdims=True))
        firsts = jnp.dot(factors, terms.astype(bf16), preferred_element_type=f32)
        out_ref[0, y : y + 1, :] = log_total
        moments = (firsts[0:4] + firsts[4:8]) / firsts[8:9]
        for k in range(4):
            out_ref[1 + k, y : y + 1, :] = moments[k : k + 1]


def shards(volume, templates, prior_table, moment_table):
    rows, cols, z_cells = volume.shape
    orients = templates.shape[0]
    n_ori = lax.axis_size("ori")
    n_ty = lax.axis_size("ty")
    own = cols // n_ori
    pairs = (own + 1) // 2
    lanes = max(128, n_ori * orients)
    vmem = pl.BlockSpec(memory_space=pltpu.VMEM)
    dma = pltpu.SemaphoreType.DMA
    out = pl.pallas_call(
        functools.partial(kernel, n_ori, n_ty, own),
        out_shape=jax.ShapeDtypeStruct((5, rows, pairs * 128), f32),
        in_specs=[vmem] * 4,
        out_specs=vmem,
        scratch_shapes=[
            pltpu.VMEM((3 * rows, 2 * cols + 3 * EDGE, z_cells), f32),
            pltpu.VMEM((n_ori, orients, 1728), bf16),
            pltpu.VMEM((n_ori, 8, lanes), f32),
            pltpu.VMEM((128, 12 * 128), bf16),
            pltpu.VMEM((rows + 11, 12, 16, pairs * 128), bf16),
            pltpu.VMEM((n_ori * orients, 2304), bf16),
            dma((5,)), dma((5,)),
            dma((n_ori - 1,)), dma((n_ori - 1,)),
            dma((n_ori - 1,)), dma((n_ori - 1,)),
        ],
        compiler_params=pltpu.CompilerParams(
            collective_id=0, has_side_effects=True, vmem_limit_bytes=48 * 2**20
        ),
    )(volume, templates, prior_table.reshape(1, orients), moment_table)
    out = out[:, :, : own * z_cells].reshape(5, rows, own, z_cells)
    return out[0], out[1:]


def solution(mesh):
    in_specs = (P(("grp", "ty"), "tx", None), P(("grp", "ori"), None), P("ori"), P(None, "ori"))
    out_specs = (P(("grp", "ty"), ("tx", "ori"), None), P(None, ("grp", "ty"), ("tx", "ori"), None))
    return jax.shard_map(shards, mesh=mesh, in_specs=in_specs, out_specs=out_specs, check_vma=False)
```

profile of v0, /device:TPU:0, one launch (start us, length us, event | category | flops | bytes accessed | tf_op | source)
XLA Modules:
  0.0 20.7 jit_solution(15016509177282912346)
XLA Ops:
  0.6 0.0 copy-start.3
  0.6 0.6 %copy-done.3 = s32[16]{0:T(128)S(1)} copy-done((s32[16]{0:T(128)S(1)}, s32[16]{0:T(128)}, u32[]{:S(2)}) %copy-start.3) | copy-done | bytes 88
  1.3 0.0 copy-start
  1.3 0.8 %copy-done = f32[8,16,64]{2,1,0:T(8,128)S(1)} copy-done((f32[8,16,64]{2,1,0:T(8,128)S(1)}, f32[8,16,64]{2,1,0:T(8,128)}, u32[]{:S(2)}) %copy-start) | copy-done | bytes 32792
  2.1 0.0 copy-start.1
  2.1 0.8 %copy-done.1 = bf16[16,1728]{1,0:T(8,128)(2,1)S(1)} copy-done((bf16[16,1728]{1,0:T(8,128)(2,1)S(1)}, bf16[16,1728]{1,0:T(8,128)(2,1)}, u32[]{:S(2)}) %copy-start.1) | copy-done | bytes 55320
  2.9 0.0 copy-start.2
  2.9 0.7 %copy-done.2 = f32[4,16]{1,0:T(4,128)S(1)} copy-done((f32[4,16]{1,0:T(4,128)S(1)}, f32[4,16]{1,0:T(4,128)}, u32[]{:S(2)}) %copy-start.2) | copy-done | bytes 280
  3.6 15.6 %shard_map.59 = f32[5,8,256]{2,1,0:T(8,128)S(1)} custom-call(f32[8,16,64]{2,1,0:T(8,128)S(1)} %copy-done, bf16[16,1728]{1,0:T(8,128)(2,1)S(1)} %copy-done.1, s32[1,16]{1,0:T(1,128)S(1)} %bitcast.1, f32[4,16]{1,0:T(4,128)S(1)} %copy-done.2), custom_call_target="tpu_custom_call" | custom-call | tf_op jit(solution)/shard_map/pallas_call | solution.py:248
  19.3 0.7 %squeeze.3 = f32[8,4,64]{2,1,0:T(4,128)} reshape(f32[1,8,256]{2,1,0:T(8,128)S(1)} %slice.10) | data formatting | bytes 16384 | tf_op jit(solution)/shard_map/squeeze | solution.py:269
  20.0 0.7 %slice.12 = f32[4,8,4,64]{3,2,1,0:T(4,128)} reshape(f32[4,8,256]{2,1,0:T(8,128)S(1)} %slice.11) | data formatting | bytes 65536 | tf_op jit(solution)/shard_map/slice | solution.py:269
  (2 shorter events, 0.0 us)
Async XLA Ops:
  0.6 0.7 %copy-start.3 = (s32[16]{0:T(128)S(1)}, s32[16]{0:T(128)}, u32[]{:S(2)}) copy-start(s32[16]{0:T(128)} %param.6) | copy-start | bytes 196
  1.3 0.8 %copy-start = (f32[8,16,64]{2,1,0:T(8,128)S(1)}, f32[8,16,64]{2,1,0:T(8,128)}, u32[]{:S(2)}) copy-start(f32[8,16,64]{2,1,0:T(8,128)} %vol_ref.1) | copy-start | bytes 98308
  2.1 0.8 %copy-start.1 = (bf16[16,1728]{1,0:T(8,128)(2,1)S(1)}, bf16[16,1728]{1,0:T(8,128)(2,1)}, u32[]{:S(2)}) copy-start(bf16[16,1728]{1,0:T(8,128)(2,1)} %tmpl_ref.1) | copy-start | bytes 165892
  2.9 0.7 %copy-start.2 = (f32[4,16]{1,0:T(4,128)S(1)}, f32[4,16]{1,0:T(4,128)}, u32[]{:S(2)}) copy-start(f32[4,16]{1,0:T(4,128)} %mom_ref.1) | copy-start | bytes 772
where the time goes:
time: 20.9 us; the launch traced here: 20.7 us
  Pallas kernels  15.6 us (75%)
  local copies, waits for them, and re-layouts  4.4 us (21%)
  between operations  0.67 us (3%)
    pallas_call x1, Pallas kernels, shards(): pl.pallas_call(functools.partial(kernel, n_ori, n_ty, own), out_shape=jax...  15.6 us
    unnamed x8, local copies, waits for them, and re-layouts  2.99 us
    slice x3, local copies, waits for them, and re-layouts, shards(): return (out[0], out[1:])  0.73 us
    squeeze x1, local copies, waits for them, and re-layouts, shards(): return (out[0], out[1:])  0.68 us

commit v1 on v0

--- a/solution.py
+++ b/solution.py
@@ -23,8 +23,9 @@
 
 def kernel(
     n_ori, n_ty, own,
-    vol_ref, tmpl_ref, prior_ref, mom_ref, out_ref,
-    ext, tall, aux, shifts, grid_ref, weights,
+    vol_ref, tmpl_ref, prior_ref, mom_ref, log_ref, mean_ref,
+    ext, tall, aux, shifts, grid_ref, weights, prior_in, mom_in,
+    local_sem,
     vol_send, vol_recv, tmpl_send, tmpl_recv, aux_send, aux_recv,
 ):
     rows, cols, z_cells = vol_ref.shape
@@ -37,6 +38,16 @@
     has_next = ty < n_ty - 1
     other = 1 - tx
     pairs = (own + 1) // 2
+    own_cols = pl.ds(pl.multiple_of(EDGE + tx * cols, 8), cols)
+    own_copies = [
+        pltpu.make_async_copy(src, dst, local_sem.at[i])
+        for i, (src, dst) in enumerate((
+            (mom_ref, mom_in),
+            (prior_ref, prior_in),
+            (vol_ref, ext.at[pl.ds(rows, rows), own_cols, :]),
+            (tmpl_ref, tall.at[ori]),
+        ))
+    ]
 
     barrier = pltpu.get_barrier_semaphore()
     for k in range(1, n_ori):
@@ -59,13 +70,16 @@
             barrier, inc=1, device_id={"ty": ty + 1, "tx": other}, device_id_type=MESH
         )
 
+    for copy in own_copies:
+        copy.start()
     lanes = aux.shape[2]
     place = (iota((orients, lanes), 1) == iota((orients, lanes), 0) + ori * orients).astype(f32)
+    own_copies[0].wait()
+    own_copies[1].wait()
     small = jnp.concatenate(
-        [mom_ref[...], prior_ref[...].astype(f32), jnp.zeros((3, orients), f32)], axis=0
+        [mom_in[...], prior_in[...].astype(f32), jnp.zeros((3, orients), f32)], axis=0
     )
     aux[ori] = jnp.dot(small, place, precision=lax.Precision.HIGHEST, preferred_element_type=f32)
-    own_cols = pl.ds(pl.multiple_of(EDGE + tx * cols, 8), cols)
 
     greeted = n_ori + jnp.where(has_prev, 2, 0) + jnp.where(has_next, 2, 0)
     pl.semaphore_wait(barrier, greeted)
@@ -114,8 +128,6 @@
             copy.start()
             gathers.append(copy)
 
-    tall[ori] = tmpl_ref[...]
-    ext[pl.ds(rows, rows), own_cols, :] = vol_ref[...]
     edge = jnp.zeros((3 * rows, EDGE, z_cells), f32)
     ext[:, 0:EDGE, :] = edge
     ext[:, EDGE + 2 * cols : EDGE + 2 * cols + EDGE, :] = edge
@@ -143,6 +155,15 @@
         (row_id == 144 * half + tap_b * 12 + (within >> 4)) & (tap_b < 12)
     ).astype(f32).astype(bf16)
 
+    group = min(4, rows // 2)
+    for g in range(group):
+        band = slice(g * all_orients, (g + 1) * all_orients)
+        if g:
+            weights[band, 0 : g * 384] = jnp.zeros((all_orients, g * 384), bf16)
+        if g < group - 1:
+            weights[band, (6 + g) * 384 :] = jnp.zeros((all_orients, (group - 1 - g) * 384), bf16)
+    own_copies[2].wait()
+    own_copies[3].wait()
     to_core.wait()
 
     @pl.when(has_next)
@@ -210,9 +231,11 @@
         copy.wait()
     cubes = tall[...].reshape(all_orients, 1728)
     for a in range(6):
-        weights[:, a * 384 : (a + 1) * 384] = jnp.dot(
+        tap = jnp.dot(
             cubes[:, a * 288 : (a + 1) * 288], perm, preferred_element_type=f32
         ).astype(bf16)
+        for g in range(group):
+            weights[g * all_orients : (g + 1) * all_orients, (a + g) * 384 : (a + g + 1) * 384] = tap
     table = jnp.sum(aux[...], axis=0)[:, 0:all_orients]
     eye = iota((all_orients, all_orients), 0) == iota((all_orients, all_orients), 1)
     prior = jnp.sum(jnp.where(eye, table[4:5], 0.0), axis=1, keepdims=True) * prior_step
@@ -221,18 +244,22 @@
     factors = jnp.concatenate(
         [high.astype(f32), low.astype(f32), jnp.ones((8, all_orients), f32)], axis=0
     ).astype(bf16)
-    for y in range(rows):
-        window = grid_ref[y : y + 12].reshape(2304, pairs * 128)
-        corr = jnp.dot(weights[...], window, preferred_element_type=f32)
-        scores = score_scale * corr - prior
-        peak = jnp.max(scores, axis=0, keepdims=True)
-        terms = jnp.exp(scores - peak)
-        log_total = peak + jnp.log(jnp.sum(terms, axis=0, keepdims=True))
-        firsts = jnp.dot(factors, terms.astype(bf16), preferred_element_type=f32)
-        out_ref[0, y : y + 1, :] = log_total
-        moments = (firsts[0:4] + firsts[4:8]) / firsts[8:9]
-        for k in range(4):
-            out_ref[1 + k, y : y + 1, :] = moments[k : k + 1]
+    depth = (2 * group + 10) * 192
+    for first in range(0, rows, 2 * group):
+        for start in (first, first + 1):
+            window = grid_ref[start : start + 2 * group + 10].reshape(depth, pairs * 128)
+            corr = jnp.dot(weights[...], window, preferred_element_type=f32)
+            for g in range(group):
+                y = start + 2 * g
+                scores = score_scale * corr[g * all_orients : (g + 1) * all_orients] - prior
+                peak = jnp.max(scores, axis=0, keepdims=True)
+                terms = jnp.exp(scores - peak)
+                log_total = peak + jnp.log(jnp.sum(terms, axis=0, keepdims=True))
+                firsts = jnp.dot(factors, terms.astype(bf16), preferred_element_type=f32)
+                moments = (firsts[0:4] + firsts[4:8]) / firsts[8:9]
+                log_ref[y : y + 1, :] = log_total
+                for k in range(4):
+                    mean_ref[k, y : y + 1, :] = moments[k : k + 1]
 
 
 def shards(volume, templates, prior_table, moment_table):
@@ -242,31 +269,40 @@
     n_ty = lax.axis_size("ty")
     own = cols // n_ori
     pairs = (own + 1) // 2
+    group = min(4, rows // 2)
     lanes = max(128, n_ori * orients)
     vmem = pl.BlockSpec(memory_space=pltpu.VMEM)
     dma = pltpu.SemaphoreType.DMA
     out = pl.pallas_call(
         functools.partial(kernel, n_ori, n_ty, own),
-        out_shape=jax.ShapeDtypeStruct((5, rows, pairs * 128), f32),
-        in_specs=[vmem] * 4,
-        out_specs=vmem,
+        out_shape=(
+            jax.ShapeDtypeStruct((rows, pairs * 128), f32),
+            jax.ShapeDtypeStruct((4, rows, pairs * 128), f32),
+        ),
+        in_specs=[pl.BlockSpec(memory_space=pltpu.HBM)] * 4,
+        out_specs=(vmem, vmem),
         scratch_shapes=[
             pltpu.VMEM((3 * rows, 2 * cols + 3 * EDGE, z_cells), f32),
             pltpu.VMEM((n_ori, orients, 1728), bf16),
             pltpu.VMEM((n_ori, 8, lanes), f32),
             pltpu.VMEM((128, 12 * 128), bf16),
             pltpu.VMEM((rows + 11, 12, 16, pairs * 128), bf16),
-            pltpu.VMEM((n_ori * orients, 2304), bf16),
+            pltpu.VMEM((group * n_ori * orients, (2 * group + 10) * 192), bf16),
+            pltpu.VMEM((1, orients), jnp.int32),
+            pltpu.VMEM((4, orients), f32),
+            dma((4,)),
             dma((5,)), dma((5,)),
             dma((n_ori - 1,)), dma((n_ori - 1,)),
             dma((n_ori - 1,)), dma((n_ori - 1,)),
         ],
         compiler_params=pltpu.CompilerParams(
-            collective_id=0, has_side_effects=True, vmem_limit_bytes=48 * 2**20
+            collective_id=0, has_side_effects=True, vmem_limit_bytes=60 * 2**20
         ),
     )(volume, templates, prior_table.reshape(1, orients), moment_table)
-    out = out[:, :, : own * z_cells].reshape(5, rows, own, z_cells)
-    return out[0], out[1:]
+    return (
+        out[0][:, : own * z_cells].reshape(rows, own, z_cells),
+        out[1][:, :, : own * z_cells].reshape(4, rows, own, z_cells),
+    )
 
 
 def solution(mesh):

time: 20.9 us -> 17.9 us (0.86)
  local copies, waits for them, and re-layouts: 4.4 us -> 2.17 us
  Pallas kernels: 15.6 us -> 14.9 us
    unnamed x8 -> x2, local copies, waits for them, and re-layouts: 2.99 us -> 0.01 us
    reshape x0 -> x2, local copies, waits for them, and re-layouts: none -> 2.16 us  [the longest x1 1.48 us: shards(): out[1][:, :, :own * z_cells].reshape(4, rows, own, z_cells)]
    pallas_call x1, Pallas kernels: 15.6 us -> 14.9 us  [shards(): pl.pallas_call(functools.partial(kernel, n_ori, n_ty, own), out_shape=(ja...]
    slice x3 -> x0, local copies, waits for them, and re-layouts: 0.73 us -> none  [shards(): return (out[0], out[1:])]
    squeeze x1 -> x0, local copies, waits for them, and re-layouts: 0.68 us -> none  [shards(): return (out[0], out[1:])]
where the time goes in v1:
time: 17.9 us; the launch traced here: 17.7 us
  Pallas kernels  14.9 us (83%)
  local copies, waits for them, and re-layouts  2.17 us (12%)
  between operations  0.65 us (4%)
    pallas_call x1, Pallas kernels, shards(): pl.pallas_call(functools.partial(kernel, n_ori, n_ty, own), out_shape=(ja...  14.9 us
    reshape x1, local copies, waits for them, and re-layouts, shards(): out[1][:, :, :own * z_cells].reshape(4, rows, own, z_cells)  1.48 us
    reshape x1, local copies, waits for them, and re-layouts, shards(): out[0][:, :own * z_cells].reshape(rows, own, z_cells)  0.68 us

profile of v1, /device:TPU:0, one launch (start us, length us, event | category | flops | bytes accessed | tf_op | source)
XLA Modules:
  0.0 17.7 jit_solution(17444424434214532360)
XLA Ops:
  0.6 14.9 %shard_map.59 = (f32[8,256]{1,0:T(8,128)}, f32[4,8,256]{2,1,0:T(8,128)}) custom-call(f32[8,16,64]{2,1,0:T(8,128)} %vol_ref.1, bf16[16,1728]{1,0:T(8,128)(2,1)} %tmpl_ref.1, s32[1,16]{1,0:T(1,128)} %bitcast.1, f32[4,16]{1,0:T(4,128)} %mom_ref.1), custom_call_target="tpu_custom_call" | custom-call | tf_op jit(solution)/shard_map/pallas_call | solution.py:276
  15.5 0.0 copy-start
  15.5 1.5 %reshape.15 = f32[4,8,4,64]{3,2,1,0:T(4,128)} reshape(f32[4,8,256]{2,1,0:T(8,128)} %get-tuple-element.5) | data formatting | bytes 65536 | tf_op jit(solution)/shard_map/reshape | solution.py:304
  17.0 0.0 copy-done
  17.0 0.7 %reshape.14 = f32[8,4,64]{2,1,0:T(4,128)} reshape(f32[8,256]{1,0:T(8,128)S(1)} %copy-done) | data formatting | bytes 16384 | tf_op jit(solution)/shard_map/reshape | solution.py:303
Async XLA Ops:
  15.5 1.5 %copy-start = (f32[8,256]{1,0:T(8,128)S(1)}, f32[8,256]{1,0:T(8,128)}, u32[]{:S(2)}) copy-start(f32[8,256]{1,0:T(8,128)} %get-tuple-element.4) | copy-start | bytes 24580

commit v2 on v1

--- a/solution.py
+++ b/solution.py
@@ -26,7 +26,7 @@
     vol_ref, tmpl_ref, prior_ref, mom_ref, log_ref, mean_ref,
     ext, tall, aux, shifts, grid_ref, weights, prior_in, mom_in,
     local_sem,
-    vol_send, vol_recv, tmpl_send, tmpl_recv, aux_send, aux_recv,
+    vol_send, vol_recv, tmpl_send, tmpl_recv, aux_send, aux_recv, core_send, core_recv,
 ):
     rows, cols, z_cells = vol_ref.shape
     orients = tmpl_ref.shape[0]
@@ -115,18 +115,39 @@
 
     to_core.start()
     gathers = []
+    direct = []
+    onward = []
+    for k in range(1, n_ori):
+        target = lax.rem(ori + k, n_ori)
+        source = lax.rem(ori + n_ori - k, n_ori)
+        direct.append((
+            lax.rem(ori + target, 2) == tx,
+            pltpu.make_async_remote_copy(
+                src_ref=tmpl_ref, dst_ref=tall.at[ori], send_sem=tmpl_send.at[k - 1],
+                recv_sem=tmpl_recv.at[k - 1], device_id={"ori": target}, device_id_type=MESH,
+            ),
+        ))
+        onward.append((
+            lax.rem(ori + source, 2) == tx,
+            pltpu.make_async_remote_copy(
+                src_ref=tmpl_ref, dst_ref=tall.at[source], send_sem=tmpl_send.at[k - 1],
+                recv_sem=tmpl_recv.at[k - 1], device_id={"ori": source}, device_id_type=MESH,
+            ),
+            pltpu.make_async_remote_copy(
+                src_ref=tall.at[source], dst_ref=tall.at[source], send_sem=core_send.at[k - 1],
+                recv_sem=core_recv.at[k - 1], device_id={"tx": other}, device_id_type=MESH,
+            ),
+        ))
     for k in sorted(range(1, n_ori), key=lambda k: -min(k, n_ori - k)):
-        target = {"ori": lax.rem(ori + k, n_ori)}
-        for src, dst, ssem, rsem in (
-            (tmpl_ref, tall.at[ori], tmpl_send, tmpl_recv),
-            (aux.at[ori], aux.at[ori], aux_send, aux_recv),
-        ):
-            copy = pltpu.make_async_remote_copy(
-                src_ref=src, dst_ref=dst, send_sem=ssem.at[k - 1], recv_sem=rsem.at[k - 1],
-                device_id=target, device_id_type=MESH,
-            )
-            copy.start()
-            gathers.append(copy)
+        pl.when(direct[k - 1][0])(direct[k - 1][1].start)
+    for k in range(1, n_ori):
+        copy = pltpu.make_async_remote_copy(
+            src_ref=aux.at[ori], dst_ref=aux.at[ori], send_sem=aux_send.at[k - 1],
+            recv_sem=aux_recv.at[k - 1], device_id={"ori": lax.rem(ori + k, n_ori)},
+            device_id_type=MESH,
+        )
+        copy.start()
+        gathers.append(copy)
 
     edge = jnp.zeros((3 * rows, EDGE, z_cells), f32)
     ext[:, 0:EDGE, :] = edge
@@ -209,6 +230,13 @@
     inside = (y_at >= 0) & (y_at < n_ty * rows) & (x_glob >= 0) & (x_glob < 2 * cols)
     inside = inside & (x_at < own + 11) & (iota(flat.shape, 2) < z_cells)
     normed = jnp.where(inside, normed, 0.0).astype(bf16).astype(f32)
+    for mine, arrival, forward in onward:
+
+        @pl.when(mine)
+        def _(arrival=arrival, forward=forward):
+            arrival.wait_recv()
+            forward.start()
+
     blocks = []
     for p in range(pairs):
         block = normed[:, 2 * p : 2 * p + 16, :]
@@ -229,6 +257,11 @@
 
     for copy in gathers:
         copy.wait()
+    for leaves, copy in direct:
+        pl.when(leaves)(copy.wait_send)
+    for mine, arrival, forward in onward:
+        pl.when(mine)(forward.wait_send)
+        pl.when(jnp.logical_not(mine))(forward.wait_recv)
     cubes = tall[...].reshape(all_orients, 1728)
     for a in range(6):
         tap = jnp.dot(
@@ -294,6 +327,7 @@
             dma((5,)), dma((5,)),
             dma((n_ori - 1,)), dma((n_ori - 1,)),
             dma((n_ori - 1,)), dma((n_ori - 1,)),
+            dma((n_ori - 1,)), dma((n_ori - 1,)),
         ],
         compiler_params=pltpu.CompilerParams(
             collective_id=0, has_side_effects=True, vmem_limit_bytes=60 * 2**20

time: 17.9 us -> 17.5 us (0.978)
  Pallas kernels: 14.9 us -> 14.4 us
    pallas_call x1, Pallas kernels: 14.9 us -> 14.4 us  [shards(): pl.pallas_call(functools.partial(kernel, n_ori, n_ty, own), out_shape=(ja...]
where the time goes in v2:
time: 17.5 us; the launch traced here: 17.2 us
  Pallas kernels  14.4 us (82%)
  local copies, waits for them, and re-layouts  2.17 us (12%)
  between operations  0.65 us (4%)
    pallas_call x1, Pallas kernels, shards(): pl.pallas_call(functools.partial(kernel, n_ori, n_ty, own), out_shape=(ja...  14.4 us
    reshape x1, local copies, waits for them, and re-layouts, shards(): out[1][:, :, :own * z_cells].reshape(4, rows, own, z_cells)  1.48 us
    reshape x1, local copies, waits for them, and re-layouts, shards(): out[0][:, :own * z_cells].reshape(rows, own, z_cells)  0.68 us

profile of v2, /device:TPU:0, one launch (start us, length us, event | category | flops | bytes accessed | tf_op | source)
XLA Modules:
  0.0 17.2 jit_solution(11717226566158085768)
XLA Ops:
  0.6 14.4 %shard_map.59 = (f32[8,256]{1,0:T(8,128)}, f32[4,8,256]{2,1,0:T(8,128)}) custom-call(f32[8,16,64]{2,1,0:T(8,128)} %vol_ref.1, bf16[16,1728]{1,0:T(8,128)(2,1)} %tmpl_ref.1, s32[1,16]{1,0:T(1,128)} %bitcast.1, f32[4,16]{1,0:T(4,128)} %mom_ref.1), custom_call_target="tpu_custom_call" | custom-call | tf_op jit(solution)/shard_map/pallas_call | solution.py:309
  15.1 0.0 copy-start
  15.1 1.5 %reshape.15 = f32[4,8,4,64]{3,2,1,0:T(4,128)} reshape(f32[4,8,256]{2,1,0:T(8,128)} %get-tuple-element.5) | data formatting | bytes 65536 | tf_op jit(solution)/shard_map/reshape | solution.py:338
  16.6 0.0 copy-done
  16.6 0.7 %reshape.14 = f32[8,4,64]{2,1,0:T(4,128)} reshape(f32[8,256]{1,0:T(8,128)S(1)} %copy-done) | data formatting | bytes 16384 | tf_op jit(solution)/shard_map/reshape | solution.py:337
Async XLA Ops:
  15.1 1.5 %copy-start = (f32[8,256]{1,0:T(8,128)S(1)}, f32[8,256]{1,0:T(8,128)}, u32[]{:S(2)}) copy-start(f32[8,256]{1,0:T(8,128)} %get-tuple-element.4) | copy-start | bytes 24580

commit v3 on v2

--- a/solution.py
+++ b/solution.py
@@ -176,7 +176,7 @@
         (row_id == 144 * half + tap_b * 12 + (within >> 4)) & (tap_b < 12)
     ).astype(f32).astype(bf16)
 
-    group = min(4, rows // 2)
+    group = min(2, rows // 2)
     for g in range(group):
         band = slice(g * all_orients, (g + 1) * all_orients)
         if g:
@@ -204,6 +204,13 @@
         to_prev_x.wait_send()
         to_next_in.wait_recv()
         to_next_x_in.wait_recv()
+
+    for mine, arrival, forward in onward:
+
+        @pl.when(mine)
+        def _(arrival=arrival, forward=forward):
+            arrival.wait_recv()
+            forward.start()
 
     grid_rows = rows + 11
     x_first = tx * cols + ori * own
@@ -230,13 +237,6 @@
     inside = (y_at >= 0) & (y_at < n_ty * rows) & (x_glob >= 0) & (x_glob < 2 * cols)
     inside = inside & (x_at < own + 11) & (iota(flat.shape, 2) < z_cells)
     normed = jnp.where(inside, normed, 0.0).astype(bf16).astype(f32)
-    for mine, arrival, forward in onward:
-
-        @pl.when(mine)
-        def _(arrival=arrival, forward=forward):
-            arrival.wait_recv()
-            forward.start()
-
     blocks = []
     for p in range(pairs):
         block = normed[:, 2 * p : 2 * p + 16, :]
@@ -302,7 +302,7 @@
     n_ty = lax.axis_size("ty")
     own = cols // n_ori
     pairs = (own + 1) // 2
-    group = min(4, rows // 2)
+    group = min(2, rows // 2)
     lanes = max(128, n_ori * orients)
     vmem = pl.BlockSpec(memory_space=pltpu.VMEM)
     dma = pltpu.SemaphoreType.DMA
@@ -330,7 +330,7 @@
             dma((n_ori - 1,)), dma((n_ori - 1,)),
         ],
         compiler_params=pltpu.CompilerParams(
-            collective_id=0, has_side_effects=True, vmem_limit_bytes=60 * 2**20
+            collective_id=0, has_side_effects=True, vmem_limit_bytes=55160 * 1024
         ),
     )(volume, templates, prior_table.reshape(1, orients), moment_table)
     return (

time: 17.5 us -> 16.6 us (0.949)
  Pallas kernels: 14.4 us -> 13 us
  local copies, waits for them, and re-layouts: 2.17 us -> 2.73 us
    pallas_call x1, Pallas kernels: 14.4 us -> 13 us  [shards(): pl.pallas_call(functools.partial(kernel, n_ori, n_ty, own), out_shape=(ja...]
    unnamed x2 -> x4, local copies, waits for them, and re-layouts: 0.01 us -> 1.33 us
    reshape x1, local copies, waits for them, and re-layouts: 1.48 us -> 0.72 us  [shards(): out[1][:, :, :own * z_cells].reshape(4, rows, own, z_cells)]
where the time goes in v3:
time: 16.6 us; the launch traced here: 16.4 us
  Pallas kernels  13 us (78%)
  local copies, waits for them, and re-layouts  2.73 us (16%)
  between operations  0.65 us (4%)
    pallas_call x1, Pallas kernels, shards(): pl.pallas_call(functools.partial(kernel, n_ori, n_ty, own), out_shape=(ja...  13 us
    unnamed x4, local copies, waits for them, and re-layouts  1.33 us
    reshape x1, local copies, waits for them, and re-layouts, shards(): out[1][:, :, :own * z_cells].reshape(4, rows, own, z_cells)  0.72 us
    reshape x1, local copies, waits for them, and re-layouts, shards(): out[0][:, :own * z_cells].reshape(rows, own, z_cells)  0.68 us

profile of v3, /device:TPU:0, one launch (start us, length us, event | category | flops | bytes accessed | tf_op | source)
XLA Modules:
  0.0 16.4 jit_solution(2056020827030778078)
XLA Ops:
  0.6 0.0 copy-start.1
  0.6 0.6 %copy-done.1 = s32[16]{0:T(128)S(1)} copy-done((s32[16]{0:T(128)S(1)}, s32[16]{0:T(128)}, u32[]{:S(2)}) %copy-start.1) | copy-done | bytes 88
  1.3 0.0 copy-start
  1.3 0.7 %copy-done = f32[4,16]{1,0:T(4,128)S(1)} copy-done((f32[4,16]{1,0:T(4,128)S(1)}, f32[4,16]{1,0:T(4,128)}, u32[]{:S(2)}) %copy-start) | copy-done | bytes 280
  2.0 13.0 %shard_map.59 = (f32[8,256]{1,0:T(8,128)S(1)}, f32[4,8,256]{2,1,0:T(8,128)S(1)}) custom-call(f32[8,16,64]{2,1,0:T(8,128)} %vol_ref.1, bf16[16,1728]{1,0:T(8,128)(2,1)} %tmpl_ref.1, s32[1,16]{1,0:T(1,128)S(1)} %bitcast.1, f32[4,16]{1,0:T(4,128)S(1)} %copy-done), custom_call_target="tpu_custom_call" | custom-call | tf_op jit(solution)/shard_map/pallas_call | solution.py:309
  15.0 0.7 %reshape.15 = f32[4,8,4,64]{3,2,1,0:T(4,128)} reshape(f32[4,8,256]{2,1,0:T(8,128)S(1)} %get-tuple-element.5) | data formatting | bytes 65536 | tf_op jit(solution)/shard_map/reshape | solution.py:338
  15.7 0.7 %reshape.14 = f32[8,4,64]{2,1,0:T(4,128)} reshape(f32[8,256]{1,0:T(8,128)S(1)} %get-tuple-element.4) | data formatting | bytes 16384 | tf_op jit(solution)/shard_map/reshape | solution.py:337
Async XLA Ops:
  0.6 0.7 %copy-start.1 = (s32[16]{0:T(128)S(1)}, s32[16]{0:T(128)}, u32[]{:S(2)}) copy-start(s32[16]{0:T(128)} %param.6) | copy-start | bytes 196
  1.3 0.7 %copy-start = (f32[4,16]{1,0:T(4,128)S(1)}, f32[4,16]{1,0:T(4,128)}, u32[]{:S(2)}) copy-start(f32[4,16]{1,0:T(4,128)} %mom_ref.1) | copy-start | bytes 772

commit v4 on v3

--- a/solution.py
+++ b/solution.py
@@ -237,6 +237,16 @@
     inside = (y_at >= 0) & (y_at < n_ty * rows) & (x_glob >= 0) & (x_glob < 2 * cols)
     inside = inside & (x_at < own + 11) & (iota(flat.shape, 2) < z_cells)
     normed = jnp.where(inside, normed, 0.0).astype(bf16).astype(f32)
+    for copy in gathers:
+        copy.wait()
+    table = jnp.sum(aux[...], axis=0)[:, 0:all_orients]
+    eye = iota((all_orients, all_orients), 0) == iota((all_orients, all_orients), 1)
+    prior = jnp.sum(jnp.where(eye, table[4:5], 0.0), axis=1, keepdims=True) * prior_step
+    high = table[0:4].astype(bf16)
+    low = (table[0:4] - high.astype(f32)).astype(bf16)
+    factors = jnp.concatenate(
+        [high.astype(f32), low.astype(f32), jnp.ones((8, all_orients), f32)], axis=0
+    ).astype(bf16)
     blocks = []
     for p in range(pairs):
         block = normed[:, 2 * p : 2 * p + 16, :]
@@ -255,8 +265,6 @@
                     :, e * 128 : (e + 1) * 128
                 ].reshape(grid_rows, 16, 128)
 
-    for copy in gathers:
-        copy.wait()
     for leaves, copy in direct:
         pl.when(leaves)(copy.wait_send)
     for mine, arrival, forward in onward:
@@ -269,14 +277,6 @@
         ).astype(bf16)
         for g in range(group):
             weights[g * all_orients : (g + 1) * all_orients, (a + g) * 384 : (a + g + 1) * 384] = tap
-    table = jnp.sum(aux[...], axis=0)[:, 0:all_orients]
-    eye = iota((all_orients, all_orients), 0) == iota((all_orients, all_orients), 1)
-    prior = jnp.sum(jnp.where(eye, table[4:5], 0.0), axis=1, keepdims=True) * prior_step
-    high = table[0:4].astype(bf16)
-    low = (table[0:4] - high.astype(f32)).astype(bf16)
-    factors = jnp.concatenate(
-        [high.astype(f32), low.astype(f32), jnp.ones((8, all_orients), f32)], axis=0
-    ).astype(bf16)
     depth = (2 * group + 10) * 192
     for first in range(0, rows, 2 * group):
         for start in (first, first + 1):

time: 16.6 us -> 16.7 us (level)
  no operation moved by 1% of the time
where the time goes in v4:
time: 16.7 us; the launch traced here: 16.5 us
  Pallas kernels  13.1 us (78%)
  local copies, waits for them, and re-layouts  2.73 us (16%)
  between operations  0.65 us (4%)
    pallas_call x1, Pallas kernels, shards(): pl.pallas_call(functools.partial(kernel, n_ori, n_ty, own), out_shape=(ja...  13.1 us
    unnamed x4, local copies, waits for them, and re-layouts  1.33 us
    reshape x1, local copies, waits for them, and re-layouts, shards(): out[1][:, :, :own * z_cells].reshape(4, rows, own, z_cells)  0.72 us
    reshape x1, local copies, waits for them, and re-layouts, shards(): out[0][:, :own * z_cells].reshape(rows, own, z_cells)  0.68 us

profile of v4, /device:TPU:0, one launch (start us, length us, event | category | flops | bytes accessed | tf_op | source)
XLA Modules:
  0.0 16.5 jit_solution(5235046111111818965)
XLA Ops:
  0.6 0.0 copy-start.1
  0.6 0.6 %copy-done.1 = s32[16]{0:T(128)S(1)} copy-done((s32[16]{0:T(128)S(1)}, s32[16]{0:T(128)}, u32[]{:S(2)}) %copy-start.1) | copy-done | bytes 88
  1.3 0.0 copy-start
  1.3 0.7 %copy-done = f32[4,16]{1,0:T(4,128)S(1)} copy-done((f32[4,16]{1,0:T(4,128)S(1)}, f32[4,16]{1,0:T(4,128)}, u32[]{:S(2)}) %copy-start) | copy-done | bytes 280
  2.0 13.1 %shard_map.59 = (f32[8,256]{1,0:T(8,128)S(1)}, f32[4,8,256]{2,1,0:T(8,128)S(1)}) custom-call(f32[8,16,64]{2,1,0:T(8,128)} %vol_ref.1, bf16[16,1728]{1,0:T(8,128)(2,1)} %tmpl_ref.1, s32[1,16]{1,0:T(1,128)S(1)} %bitcast.1, f32[4,16]{1,0:T(4,128)S(1)} %copy-done), custom_call_target="tpu_custom_call" | custom-call | tf_op jit(solution)/shard_map/pallas_call | solution.py:309
  15.1 0.7 %reshape.15 = f32[4,8,4,64]{3,2,1,0:T(4,128)} reshape(f32[4,8,256]{2,1,0:T(8,128)S(1)} %get-tuple-element.5) | data formatting | bytes 65536 | tf_op jit(solution)/shard_map/reshape | solution.py:338
  15.8 0.7 %reshape.14 = f32[8,4,64]{2,1,0:T(4,128)} reshape(f32[8,256]{1,0:T(8,128)S(1)} %get-tuple-element.4) | data formatting | bytes 16384 | tf_op jit(solution)/shard_map/reshape | solution.py:337
Async XLA Ops:
  0.6 0.7 %copy-start.1 = (s32[16]{0:T(128)S(1)}, s32[16]{0:T(128)}, u32[]{:S(2)}) copy-start(s32[16]{0:T(128)} %param.6) | copy-start | bytes 196
  1.3 0.7 %copy-start = (f32[4,16]{1,0:T(4,128)S(1)}, f32[4,16]{1,0:T(4,128)}, u32[]{:S(2)}) copy-start(f32[4,16]{1,0:T(4,128)} %mom_ref.1) | copy-start | bytes 772
